TPU v7x, 32 devices: a whole 2x2x4 slice. The times are simulated.
32 devices in a mesh: tm: 16 (over z, y, x), row: 2 (over core).
Axes of the slice: x: 2, y: 2, z: 4, core: 2. Of those that a mesh axis runs over, the one named last changes fastest.
Arguments:
- trans: bfloat16 [32, 1024, 1024], P('tm', 'row'), may hold values from -0.3 to 0.9
- offset: bfloat16 [32, 1024], P('tm', 'row'), may hold values from -6 to 6
- spread: bfloat16 [32, 1024, 1024], P('tm', 'row'), may hold values from -0.3 to 2.3, as said below
Outputs:
- trans_out: bfloat16 [32, 1024, 1024], P('tm', 'row')
- offset_out: bfloat16 [32, 1024], P('tm', 'row')
- spread_out: bfloat16 [32, 1024, 1024], P('tm', 'row')
Inputs may be any that keep to these rules, and one draw needn't show every extreme that they name: `spread`: each block's matrix is symmetric.
All inputs are finite; a program needn't handle non-finite values.
Results may differ from a plain program's by a relative error of at most 0.0056.
Values may be sent and summed in bfloat16 or wider, within the bound.
A program may use at most 64 MiB of HBM per device.

v0:
```python
import jax
import jax.numpy as jnp
from jax import lax
from jax.sharding import PartitionSpec as P


def from_later(block, distance):
    devices = range(lax.axis_size("tm"))
    route = [(i, i - distance) for i in devices if i - distance in devices]
    return lax.ppermute(block, "tm", route)


def rows_of_all(block):
    return lax.all_gather(block, "row", axis=0, tiled=True)


def product(a, b):
    return jnp.dot(a, b, preferred_element_type=jnp.float32)


def compose(own, own_trans_full, later_full):
    trans, offset, spread = own
    far_trans, far_offset, far_spread = later_full
    mixed_trans = product(trans, far_trans).astype(jnp.bfloat16)
    mixed_offset = (product(trans, far_offset) + offset.astype(jnp.float32)).astype(jnp.bfloat16)
    partial_value = product(trans, far_spread).astype(jnp.bfloat16)
    mixed_spread = jnp.einsum("ik,jk->ij", partial_value, own_trans_full, preferred_element_type=jnp.float32)
    mixed_spread = (mixed_spread + spread.astype(jnp.float32)).astype(jnp.bfloat16)
    return mixed_trans, mixed_offset, mixed_spread


def on_device(trans, offset, spread):
    count = lax.axis_size("tm")
    position = lax.axis_index("tm")
    zero = (trans[0], offset[0], spread[0])
    one = (trans[1], offset[1], spread[1])
    four = from_later(zero, 2)
    one_full = tuple(rows_of_all(x) for x in one)
    zero_trans_full = rows_of_all(trans[0])
    pair = compose(zero, zero_trans_full, one_full)
    next_pair = from_later(pair, 1)
    four_full = tuple(rows_of_all(x) for x in four)
    pair_trans_full = rows_of_all(pair[0])
    next_full = tuple(rows_of_all(x) for x in next_pair)
    triple = compose(one, one_full[0], next_full)
    triple_trans_full = rows_of_all(triple[0])
    first = compose(pair, pair_trans_full, next_full)
    second = compose(triple, triple_trans_full, four_full)
    is_last = position == count - 1
    is_before = position == count - 2
    first = tuple(jnp.where(is_last, a, b) for a, b in zip(pair, first))
    second = tuple(jnp.where(is_last, a, jnp.where(is_before, b, c)) for a, b, c in zip(one, triple, second))
    return tuple(jnp.stack([a, b]) for a, b in zip(first, second))


def solution(mesh):
    placed = (P("tm", "row", None), P("tm", "row"), P("tm", "row", None))
    return jax.shard_map(on_device, mesh=mesh, in_specs=placed, out_specs=placed, check_vma=False)
```

profile of v0, /device:TPU:7, one launch (start us, length us, event | category | flops | bytes accessed | tf_op | source)
XLA Modules:
  0.0 198.2 jit_solution(8141906460418974650)
XLA Ops:
  7.2 3.5 %fusion.55 = (bf16[1,512,1024]{2,1,0:T(8,128)(2,1)}, bf16[512,1024]{1,0:T(8,128)(2,1)}, bf16[1,512,1024]{2,1,0:T(8,128)(2,1)}) fusion(bf16[2,512,1024]{2,1,0:T(8,128)(2,1)} %param.3), kind=kLoop, calls=%fused_computation.61 | loop fusion | bytes 5242880 | tf_op jit(solution)/shard_map/slice | solution.py:35
  10.8 0.7 all-gather.32.cloned.1.call-update
  11.6 3.2 %slice_bitcast_fusion = (bf16[512,1024]{1,0:T(8,128)(2,1)}, bf16[1,512,1024]{2,1,0:T(8,128)(2,1)}) fusion(bf16[2,512,1024]{2,1,0:T(8,128)(2,1)} %param.5), kind=kLoop, calls=%fused_computation.36 | loop fusion | bytes 4194304 | tf_op jit(solution)/shard_map/squeeze | solution.py:35
  14.8 8.5 %all-gather.28.cloned.1.call-done = bf16[1,1024,1024]{2,1,0:T(8,128)(2,1)} async-done(((bf16[1,512,1024]{2,1,0:T(8,128)(2,1)}), bf16[1,1024,1024]{2,1,0:T(8,128)(2,1)}) %all-gather.28.cloned.1.call-update) | async-done | bytes 2097168 | tf_op jit(solution)/shard_map/all_gather | solution.py:14
  23.4 2.8 %fusion.14 = bf16[512,1024]{1,0:T(8,128)(2,1)S(1)} fusion(bf16[1,1024,1024]{2,1,0:T(8,128)(2,1)} %all-gather.28.cloned.1.call-done, bf16[2,512,1024]{2,1,0:T(8,128)(2,1)S(1)} %copy-done), kind=kOutput, calls=%fused_computation.16 | convolution fusion | flops 1074266112 | bytes 4194304 | tf_op jit(solution)/shard_map/dot_general | solution.py:18
  26.3 2.2 %collective-permute-start = (bf16[512,1024]{1,0:T(8,128)(2,1)S(1)}, bf16[512,1024]{1,0:T(8,128)(2,1)}, u32[]{:S(2)}, u32[]{:S(2)}) collective-permute-start(bf16[512,1024]{1,0:T(8,128)(2,1)S(1)} %fusion.14), channel_id=1, source_target_pairs={{2,0},{4,2},{6,4},{8,6},{10,8},{12,10},{14,12},{16,14},{18,16},{20... | collective-permute-start | bytes 3145736 | tf_op jit(solution)/shard_map/ppermute | solution.py:10
  28.4 26.2 %collective-permute-done = bf16[512,1024]{1,0:T(8,128)(2,1)} collective-permute-done((bf16[512,1024]{1,0:T(8,128)(2,1)S(1)}, bf16[512,1024]{1,0:T(8,128)(2,1)}, u32[]{:S(2)}, u32[]{:S(2)}) %collective-permute-start) | collective-permute-done | bytes 1048608 | tf_op jit(solution)/shard_map/ppermute | solution.py:10
  54.7 1.9 collective-permute-start.1
  56.6 24.8 %collective-permute-done.1 = bf16[512,1024]{1,0:T(8,128)(2,1)} collective-permute-done((bf16[512,1024]{1,0:T(8,128)(2,1)}, bf16[512,1024]{1,0:T(8,128)(2,1)}, u32[]{:S(2)}, u32[]{:S(2)}) %collective-permute-start.1) | collective-permute-done | bytes 1048608 | tf_op jit(solution)/shard_map/ppermute | solution.py:10
  81.5 5.8 %add_convert_fusion.3 = bf16[512,1024]{1,0:T(8,128)(2,1)} fusion(bf16[1,1024,1024]{2,1,0:T(8,128)(2,1)} %all-gather.32.cloned.1.call-done, bf16[1,1024,1024]{2,1,0:T(8,128)(2,1)} %all-gather.30.cloned.1.call-done, bf16[2,512,1024]{2,1,0:T(8,128)(2,1)} %param.5, bf16[2,512,1024]{2,1,0:T(8,128)(2,1)S(1)} %copy-done), kind=kOutput, calls=%fused_computation.13 | convolution fusion | flops 2149580800 | bytes 7340032 | tf_op jit(solution)/shard_map/ik,jk->ij/dot_general | solution.py:27
  87.4 2.0 %collective-permute-start.4 = (bf16[512,1024]{1,0:T(8,128)(2,1)}, bf16[512,1024]{1,0:T(8,128)(2,1)}, u32[]{:S(2)}, u32[]{:S(2)}) collective-permute-start(bf16[512,1024]{1,0:T(8,128)(2,1)} %add_convert_fusion.3), channel_id=1, source_target_pairs={{2,0},{4,2},{6,4},{8,6},{10,8},{12,10},{14,12},{16,14},{18,16},{20... | collective-permute-start | bytes 3145736 | tf_op jit(solution)/shard_map/ppermute | solution.py:10
  89.4 24.8 %collective-permute-done.4 = bf16[512,1024]{1,0:T(8,128)(2,1)} collective-permute-done((bf16[512,1024]{1,0:T(8,128)(2,1)}, bf16[512,1024]{1,0:T(8,128)(2,1)}, u32[]{:S(2)}, u32[]{:S(2)}) %collective-permute-start.4) | collective-permute-done | bytes 1048608 | tf_op jit(solution)/shard_map/ppermute | solution.py:10
  114.3 0.7 all-gather.22.cloned.1.call-update
  115.0 1.9 collective-permute-start.5
  117.0 23.0 %collective-permute-done.5 = bf16[512,1024]{1,0:T(8,128)(2,1)} collective-permute-done((bf16[512,1024]{1,0:T(8,128)(2,1)}, bf16[512,1024]{1,0:T(8,128)(2,1)}, u32[]{:S(2)}, u32[]{:S(2)}) %collective-permute-start.5) | collective-permute-done | bytes 1048608 | tf_op jit(solution)/shard_map/ppermute | solution.py:10
  140.0 1.9 collective-permute-start.3
  142.0 5.3 %all-gather.1 = bf16[1,1024]{1,0:T(2,128)(2,1)S(1)} all-gather(bf16[1,512]{1,0:T(2,128)(2,1)S(1)} %get-tuple-element.10), channel_id=3, replica_groups=mesh['tm'=16,'row'=2] {'row'}, dimensions={1}, use_global_device_ids=true | all-gather | bytes 3072 | tf_op jit(solution)/shard_map/all_gather | solution.py:14
  147.6 1.9 collective-permute-start.2
  149.6 4.2 %collective-permute-done.2 = bf16[512]{0:T(512)(128)(2,1)S(1)} collective-permute-done((bf16[512]{0:T(512)(128)(2,1)S(1)}, bf16[512]{0:T(512)(128)(2,1)S(1)}, u32[]{:S(2)}, u32[]{:S(2)}) %collective-permute-start.2) | collective-permute-done | bytes 1056 | tf_op jit(solution)/shard_map/ppermute | solution.py:10
  153.7 2.9 %all-gather.5 = bf16[2,1,512]{2,1,0:T(2,128)(2,1)S(1)} all-gather(bf16[1,1,512]{2,1,0:T(2,128)(2,1)S(1)} %reshape.12), channel_id=1, replica_groups=mesh['tm'=16,'row'=2] {'row'}, dimensions={0}, use_global_device_ids=true | all-gather | bytes 3072 | tf_op jit(solution)/shard_map/all_gather | solution.py:14
  156.6 2.0 all-gather.4
  159.0 0.4 fusion.56
  159.4 2.8 %convolution_convert_fusion = bf16[1024,512]{0,1:T(8,128)(2,1)S(1)} fusion(bf16[1024,1024]{1,0:T(8,128)(2,1)} %all-gather.16.cloned.1.call-done, bf16[2,512,1024]{2,1,0:T(8,128)(2,1)S(1)} %copy-done), kind=kOutput, calls=%fused_computation.18 | convolution fusion | flops 1074266112 | bytes 4194304 | tf_op jit(solution)/shard_map/dot_general | solution.py:18
  162.3 1.0 copy-done.3
  163.7 3.8 %fusion.21 = bf16[1,512,1024]{2,1,0:T(8,128)(2,1)} fusion(bf16[512,1024]{1,0:T(8,128)(2,1)S(1)} %copy-done.2, bf16[1024,1024]{1,0:T(8,128)(2,1)} %all-gather.16.cloned.1.call-done, pred[]{:T(512)S(6)} %eq.6), kind=kOutput, calls=%fused_computation.25 | convolution fusion | flops 1074790400 | bytes 4194305 | tf_op jit(solution)/shard_map/dot_general | solution.py:18
  167.5 0.6 pad_maximum_fusion.2
  168.1 3.5 %fusion.27 = bf16[1,512,1024]{2,1,0:T(8,128)(2,1)S(1)} fusion(bf16[1024,512]{0,1:T(8,128)(2,1)} %copy-done.3, bf16[1024,1024]{1,0:T(8,128)(2,1)} %all-gather.18.cloned.1.call-done, pred[]{:T(512)S(6)} %eq.7, pred[]{:T(512)S(6)} %eq.6, bf16[2,512,1024]{2,1,0:T(8,128)(2,1)S(1)} %copy-done), kind=kOutput, calls=%fused_computation.31 | convolution fusion | flops 1075314688 | bytes 6291458 | tf_op jit(solution)/shard_map/dot_general | solution.py:18
  171.6 1.5 pad_maximum_fusion
  173.1 5.9 %add_convert_fusion.1 = bf16[512,1024]{1,0:T(8,128)(2,1)} fusion(bf16[1,1024,1024]{2,1,0:T(8,128)(2,1)} %all-gather.28.cloned.1.call-done, bf16[1024,1024]{1,0:T(8,128)(2,1)} %all-gather.20.cloned.1.call-done, bf16[2,512,1024]{2,1,0:T(8,128)(2,1)} %param.5, bf16[2,512,1024]{2,1,0:T(8,128)(2,1)S(1)} %copy-done), kind=kOutput, calls=%fused_computation.11 | convolution fusion | flops 2149580800 | bytes 7340032 | tf_op jit(solution)/shard_map/ik,jk->ij/dot_general | solution.py:27
  179.0 5.3 %fusion.22 = bf16[1,512,1024]{2,1,0:T(8,128)(2,1)S(1)} fusion(bf16[512,1024]{1,0:T(8,128)(2,1)} %add_convert_fusion.3, bf16[1024,1024]{1,0:T(8,128)(2,1)} %all-gather.22.cloned.1.call-done, pred[]{:T(512)S(6)} %eq.6, bf16[512,1024]{1,0:T(8,128)(2,1)S(1)} %copy-done.2, bf16[1024,1024]{1,0:T(8,128)(2,1)} %all-gather.20.cloned.1.call-done), kind=kOutput, calls=%fused_computation.26 | convolution fusion | flops 2150105088 | bytes 7340033 | tf_op jit(solution)/shard_map/ik,jk->ij/dot_general | solution.py:27
  184.4 5.7 %fusion.24 = bf16[1,512,1024]{2,1,0:T(8,128)(2,1)S(1)} fusion(bf16[512,1024]{1,0:T(8,128)(2,1)} %add_convert_fusion.1, bf16[1024,1024]{1,0:T(8,128)(2,1)} %all-gather.26.cloned.1.call-done, pred[]{:T(512)S(6)} %eq.7, pred[]{:T(512)S(6)} %eq.6, bf16[1024,512]{0,1:T(8,128)(2,1)S(1)} %copy-done.4, bf16[1024,1024]{1,0:T(8,128)(2,1)} %all-gather.24.cloned.1.call-done, ...), kind=kOutput, calls=%fused_computation.28 | convolution fusion | flops 2150629376 | bytes 8388610 | tf_op jit(solution)/shard_map/ik,jk->ij/dot_general | solution.py:27
  190.1 1.5 pad_maximum_fusion.1
  (49 shorter events, 1.8 us)
Async XLA Ops:
  7.2 16.2 %all-gather.28.cloned.1.call-start = ((), (), s32[]{:S(2)}) async-start(), calls=%async_computation.6 | async-start | bytes 3145728 | tf_op jit(solution)/shard_map/all_gather | solution.py:14
  10.8 70.8 %all-gather.32.cloned.1.call-start = ((), (), s32[]{:S(2)}) async-start(), calls=%async_computation.8 | async-start | bytes 3145728 | tf_op jit(solution)/shard_map/all_gather | solution.py:14
  11.5 11.9 %copy-start = (bf16[2,512,1024]{2,1,0:T(8,128)(2,1)S(1)}, bf16[2,512,1024]{2,1,0:T(8,128)(2,1)}, u32[]{:S(2)}) copy-start(bf16[2,512,1024]{2,1,0:T(8,128)(2,1)} %param.3) | copy-start | bytes 6291460
  11.5 70.0 %all-gather.30.cloned.1.call-start = ((), (), s32[]{:S(2)}) async-start(), calls=%async_computation.7 | async-start | bytes 3145728 | tf_op jit(solution)/shard_map/all_gather | solution.py:14
  14.8 144.6 %all-gather.16.cloned.1.call-start = ((), (), s32[]{:S(2)}) async-start(), calls=%async_computation | async-start | bytes 3145728 | tf_op jit(solution)/shard_map/all_gather | solution.py:14
  26.2 61.1 %copy-start.1 = (bf16[512,1024]{1,0:T(8,128)(2,1)}, bf16[512,1024]{1,0:T(8,128)(2,1)S(1)}, u32[]{:S(2)}) copy-start(bf16[512,1024]{1,0:T(8,128)(2,1)S(1)} %fusion.14) | copy-start | bytes 3145732
  26.3 28.4 %collective-permute-start = (bf16[512,1024]{1,0:T(8,128)(2,1)S(1)}, bf16[512,1024]{1,0:T(8,128)(2,1)}, u32[]{:S(2)}, u32[]{:S(2)}) collective-permute-start(bf16[512,1024]{1,0:T(8,128)(2,1)S(1)} %fusion.14), channel_id=1, source_target_pairs={{2,0},{4,2},{6,4},{8,6},{10,8},{12,10},{14,12},{16,14},{18,16},{20... | collective-permute-start | bytes 3145736 | tf_op jit(solution)/shard_map/ppermute | solution.py:10
  54.6 113.4 %all-gather.18.cloned.1.call-start = ((), (), s32[]{:S(2)}) async-start(), calls=%async_computation.1 | async-start | bytes 3145728 | tf_op jit(solution)/shard_map/all_gather | solution.py:14
  54.7 26.7 %collective-permute-start.1 = (bf16[512,1024]{1,0:T(8,128)(2,1)}, bf16[512,1024]{1,0:T(8,128)(2,1)}, u32[]{:S(2)}, u32[]{:S(2)}) collective-permute-start(bf16[512,1024]{1,0:T(8,128)(2,1)} %get-tuple-element.8), channel_id=1, source_target_pairs={{4,0},{6,2},{8,4},{10,6},{12,8},{14,10},{16,12},{18,14},{20,16},{2... | collective-permute-start | bytes 3145736 | tf_op jit(solution)/shard_map/ppermute | solution.py:10
  81.4 91.7 %all-gather.20.cloned.1.call-start = ((), (), s32[]{:S(2)}) async-start(), calls=%async_computation.2 | async-start | bytes 3145728 | tf_op jit(solution)/shard_map/all_gather | solution.py:14
  87.4 52.6 %copy-start.6 = (bf16[2,512]{1,0:T(2,128)(2,1)S(1)}, bf16[2,512]{1,0:T(2,128)(2,1)}, u32[]{:S(2)}) copy-start(bf16[2,512]{1,0:T(2,128)(2,1)} %param.4) | copy-start | bytes 6148
  87.4 26.8 %collective-permute-start.4 = (bf16[512,1024]{1,0:T(8,128)(2,1)}, bf16[512,1024]{1,0:T(8,128)(2,1)}, u32[]{:S(2)}, u32[]{:S(2)}) collective-permute-start(bf16[512,1024]{1,0:T(8,128)(2,1)} %add_convert_fusion.3), channel_id=1, source_target_pairs={{2,0},{4,2},{6,4},{8,6},{10,8},{12,10},{14,12},{16,14},{18,16},{20... | collective-permute-start | bytes 3145736 | tf_op jit(solution)/shard_map/ppermute | solution.py:10
  114.2 44.8 %copy-start.2 = (bf16[512,1024]{1,0:T(8,128)(2,1)S(1)}, bf16[512,1024]{1,0:T(8,128)(2,1)}, u32[]{:S(2)}) copy-start(bf16[512,1024]{1,0:T(8,128)(2,1)} %copy-done.1) | copy-start | bytes 3145732
  114.2 64.8 %all-gather.22.cloned.1.call-start = ((), (), s32[]{:S(2)}) async-start(), calls=%async_computation.3 | async-start | bytes 3145728 | tf_op jit(solution)/shard_map/all_gather | solution.py:14
  115.0 69.4 %all-gather.24.cloned.1.call-start = ((), (), s32[]{:S(2)}) async-start(), calls=%async_computation.4 | async-start | bytes 3145728 | tf_op jit(solution)/shard_map/all_gather | solution.py:14
  115.0 24.9 %collective-permute-start.5 = (bf16[512,1024]{1,0:T(8,128)(2,1)}, bf16[512,1024]{1,0:T(8,128)(2,1)}, u32[]{:S(2)}, u32[]{:S(2)}) collective-permute-start(bf16[512,1024]{1,0:T(8,128)(2,1)} %get-tuple-element.5), channel_id=1, source_target_pairs={{4,0},{6,2},{8,4},{10,6},{12,8},{14,10},{16,12},{18,14},{20,16},{2... | collective-permute-start | bytes 3145736 | tf_op jit(solution)/shard_map/ppermute | solution.py:10
  140.0 44.4 %all-gather.26.cloned.1.call-start = ((), (), s32[]{:S(2)}) async-start(), calls=%async_computation.5 | async-start | bytes 3145728 | tf_op jit(solution)/shard_map/all_gather | solution.py:14
  140.0 9.5 %collective-permute-start.3 = (bf16[512]{0:T(512)(128)(2,1)S(1)}, bf16[512]{0:T(512)(128)(2,1)S(1)}, u32[]{:S(2)}, u32[]{:S(2)}) collective-permute-start(bf16[512]{0:T(512)(128)(2,1)S(1)} %get-tuple-element.3), channel_id=1, source_target_pairs={{4,0},{6,2},{8,4},{10,6},{12,8},{14,10},{16,12},{18,14},{20,16},{2... | collective-permute-start | bytes 3080 | tf_op jit(solution)/shard_map/ppermute | solution.py:10
  147.6 6.1 %collective-permute-start.2 = (bf16[512]{0:T(512)(128)(2,1)S(1)}, bf16[512]{0:T(512)(128)(2,1)S(1)}, u32[]{:S(2)}, u32[]{:S(2)}) collective-permute-start(bf16[512]{0:T(512)(128)(2,1)S(1)} %add_convert_fusion.7), channel_id=1, source_target_pairs={{2,0},{4,2},{6,4},{8,6},{10,8},{12,10},{14,12},{16,14},{18,16},{20... | collective-permute-start | bytes 3080 | tf_op jit(solution)/shard_map/ppermute | solution.py:10
  162.3 1.0 copy-start.3
  168.1 3.5 %copy-start.5 = (bf16[1,512,1024]{2,1,0:T(8,128)(2,1)S(1)}, bf16[1,512,1024]{2,1,0:T(8,128)(2,1)}, u32[]{:S(2)}) copy-start(bf16[1,512,1024]{2,1,0:T(8,128)(2,1)} %fusion.21) | copy-start | bytes 3145732
  179.0 5.4 %copy-start.4 = (bf16[1024,512]{0,1:T(8,128)(2,1)S(1)}, bf16[1024,512]{0,1:T(8,128)(2,1)}, u32[]{:S(2)}) copy-start(bf16[1024,512]{0,1:T(8,128)(2,1)} %copy-done.3) | copy-start | bytes 3145732
Sparse Core Ops, SparseCore 0:
  10.9 12.4 all-gather.27
  25.5 11.7 all-gather.31
  38.8 11.7 all-gather.29
  54.8 11.6 all-gather.15
  81.6 12.5 all-gather.17
  114.3 13.4 all-gather.19
  129.4 11.7 all-gather.21
  142.7 11.7 all-gather.23
  163.8 11.4 all-gather.25
where the time goes:
time: 199 us; the launch traced here: 198 us
  waiting for transfers between devices  113 us (57%)
  matrix products  37.2 us (19%)
  between operations  14.1 us (7%)
  starting transfers between devices  12.3 us (6%)
  blocking collectives  10.1 us (5%)
  local copies, waits for them, and re-layouts  7.77 us (4%)
  other arithmetic  3.62 us (2%)
    ppermute x6, waiting for transfers between devices, from_later(): return lax.ppermute(block, 'tm', route)  103 us
    dot_general x4, matrix products, compose(): jnp.einsum('ik,jk->ij', partial_value, own_trans_full, preferred_element_...  22.7 us
    dot_general x8, matrix products, product(): return jnp.dot(a, b, preferred_element_type=jnp.float32)  14.5 us
    ppermute x6, starting transfers between devices, from_later(): return lax.ppermute(block, 'tm', route)  11.9 us
    all_gather x3, blocking collectives, rows_of_all(): return lax.all_gather(block, 'row', axis=0, tiled=True)  10.1 us
    all_gather x9, waiting for transfers between devices, rows_of_all(): return lax.all_gather(block, 'row', axis=0, tiled=True)  8.65 us
  transfers between devices with their start and end apart: 15, of which 6 were waited for; matrix products, arithmetic and copies ran while one was open for 19% of the time, Pallas kernels for 0%

commit v1 on v0

v1 whole, which is shorter than its diff:
```python
import functools
import jax
import jax.numpy as jnp
from jax import lax
from jax.experimental import pallas as pl
from jax.experimental.pallas import tpu as pltpu
from jax.sharding import PartitionSpec as P

MESH = pl.DeviceIdType.MESH
LINES = 16
TILE = 256


def pieces(core, cores, rows, width):
    if cores != 2 or rows % 256 or width != 2 * rows:
        return [(0, rows, 0, width)]
    q = rows // 2
    return [
        (0, q, core * (2 * q), 2 * q),
        (core * q, q, (2 + core) * q, q),
        (q, q, (1 - core) * q, 2 * q),
    ]


def mirror(matrix, cores, rows, width):
    if cores != 2 or rows % 256 or width != 2 * rows:
        return
    q = rows // 2
    for i, j in ((1, 0), (2, 0), (2, 1), (3, 2), (0, 3), (1, 3)):
        block = matrix[pl.ds(j * q, q), pl.ds(i * q, q)]
        matrix[pl.ds(i * q, q), pl.ds(j * q, q)] = block.T


def kernel(
    count, cores, trans, goff, spread, out_trans, out_goff, out_spread,
    e0, e1, l1, pe, ne, nl, fe, fl, te, mixed, pl_own, tl_own, g1, ng, fg, pg, tg,
    send_sem, recv_sem,
):
    rows, width = trans.shape[1:]
    tile = min(TILE, width)
    position = lax.axis_index("tm")
    core = lax.axis_index("row")
    peers = [(k, lax.rem(core + k, cores)) for k in range(1, cores)]
    used = [0]

    barrier = pltpu.get_barrier_semaphore()
    expected = jnp.int32(cores - 1)
    for _, peer in peers:
        pl.semaphore_signal(barrier, inc=1, device_id={"row": peer}, device_id_type=MESH)
    for step in (-2, -1, 1, 2):
        there = jnp.logical_and(position + step >= 0, position + step < count)
        expected = expected + there.astype(jnp.int32)

        @pl.when(there)
        def _(step=step):
            pl.semaphore_signal(barrier, inc=1, device_id={"tm": position + step}, device_id_type=MESH)

    pl.semaphore_wait(barrier, expected)

    def remote(source, target, device):
        k = used[0]
        used[0] += 1
        return pltpu.make_async_remote_copy(
            src_ref=source, dst_ref=target, send_sem=send_sem.at[k], recv_sem=recv_sem.at[k],
            device_id=device, device_id_type=MESH,
        )

    def place(index, size):
        if isinstance(index, int):
            return pl.ds(index, size)
        return pl.ds(pl.multiple_of(index, 128), size)

    own = place(core * rows, rows)

    def spread_rows(matrix, parts, source=None):
        copies = []
        for row, n_rows, column, n_columns in parts:
            target = matrix.at[place(core * rows + row, n_rows), place(column, n_columns)]
            if source is None:
                origin = target
            else:
                origin = source.at[place(row, n_rows), place(column, n_columns)]
            copies.append((origin, target))
        return copies

    whole = [(0, rows, 0, width)]
    half = pieces(core, cores, rows, width)

    def to_device(pairs, device):
        return [remote(a, b, device) for a, b in pairs]

    def to_peers(pairs):
        return [remote(a, b, {"row": peer}) for _, peer in peers for a, b in pairs]

    def start(copies):
        for copy in copies:
            copy.start()

    def arrived(copies):
        for copy in copies:
            copy.wait_recv()

    def left(copies):
        for copy in copies:
            copy.wait_send()

    def times(a, b, out):
        @pl.loop(0, width // tile)
        def _(n):
            columns = pl.ds(pl.multiple_of(n * tile, tile), tile)
            out[:, columns] = jnp.dot(
                a[...], b[:, columns], preferred_element_type=jnp.float32
            ).astype(jnp.bfloat16)

    def times_transposed(a, b, added, out):
        @pl.loop(0, width // tile)
        def _(n):
            columns = pl.ds(pl.multiple_of(n * tile, tile), tile)
            value = lax.dot_general(
                a[...], b[columns, :], (((1,), (1,)), ((), ())), preferred_element_type=jnp.float32
            )
            out[:, columns] = (value + added[:, columns].astype(jnp.float32)).astype(jnp.bfloat16)

    def shift(a, g, added, out):
        total = added[...].astype(jnp.float32)
        for k in range(cores):
            total = total + lax.dot_general(
                g[k], a[:, pl.ds(k * rows, rows)], (((1,), (1,)), ((), ())),
                preferred_element_type=jnp.float32,
            )
        out[...] = total.astype(jnp.bfloat16)

    two = {"tm": position - 2}
    one = {"tm": position - 1}
    row_e1 = to_peers(spread_rows(e1, whole, trans.at[1]))
    row_l1 = to_peers(spread_rows(l1, whole, spread.at[1]))
    row_g1 = to_peers([(goff.at[1], g1.at[core])])
    row_e0 = to_peers(spread_rows(e0, whole, trans.at[0]))
    far_e = to_device(spread_rows(fe, whole, trans.at[0]), two)
    far_l = to_device(spread_rows(fl, half, spread.at[0]), two)
    far_g = to_device([(goff.at[0], fg.at[core])], two)
    next_e = to_device(spread_rows(ne, whole, pe.at[own, :]), one)
    next_l = to_device(spread_rows(nl, half, pl_own), one)
    next_g = to_device([(pg, ng.at[core])], one)
    row_pe = to_peers(spread_rows(pe, whole))
    row_fe = to_peers(spread_rows(fe, whole))
    row_fl = to_peers(spread_rows(fl, half))
    row_fg = to_peers([(fg.at[core], fg.at[core])])
    row_ne = to_peers(spread_rows(ne, whole))
    row_nl = to_peers(spread_rows(nl, half))
    row_ng = to_peers([(ng.at[core], ng.at[core])])
    row_te = to_peers(spread_rows(te, whole))

    gives_two = position >= 2
    gives_one = position >= 1
    takes_two = position + 2 < count
    takes_one = position + 1 < count

    start(row_e1)

    @pl.when(gives_two)
    def _():
        start(far_e + far_g + far_l)

    start(row_g1 + row_l1 + row_e0)
    e1[own, :] = trans[1]
    l1[own, :] = spread[1]
    e0[own, :] = trans[0]
    g1[core] = goff[1]

    arrived(row_e1)
    times(trans.at[0], e1, pe.at[own, :])
    start(row_pe)

    @pl.when(gives_one)
    def _():
        start(next_e)

    arrived(row_g1)
    shift(trans.at[0], g1, goff.at[0], pg)
    arrived(row_l1)
    times(trans.at[0], l1, mixed)
    arrived(row_e0)
    times_transposed(mixed, e0, spread.at[0], pl_own)

    @pl.when(gives_one)
    def _():
        start(next_g + next_l)

    arrived(row_pe)

    @pl.when(takes_two)
    def _():
        arrived(far_e)
        start(row_fe)
        arrived(far_g)
        start(row_fg)

    @pl.when(takes_one)
    def _():
        arrived(next_e)
        start(row_ne)
        arrived(next_g)
        start(row_ng)
        arrived(row_ne)
        times(trans.at[1], ne, te.at[own, :])
        start(row_te)
        times(pe.at[own, :], ne, out_trans.at[0])
        arrived(row_ng)
        shift(trans.at[1], ng, goff.at[1], tg)
        shift(pe.at[own, :], ng, pg, out_goff.at[0])

    @pl.when(takes_two)
    def _():
        arrived(far_l)
        start(row_fl)
        arrived(row_fe)
        times(te.at[own, :], fe, out_trans.at[1])
        arrived(row_fg)
        shift(te.at[own, :], fg, tg, out_goff.at[1])
        arrived(row_fl)
        mirror(fl, cores, rows, width)

    @pl.when(takes_one)
    def _():
        arrived(next_l)
        start(row_nl)
        arrived(row_nl)
        mirror(nl, cores, rows, width)
        times(pe.at[own, :], nl, mixed)
        times_transposed(mixed, pe, pl_own, out_spread.at[0])
        times(trans.at[1], nl, mixed)
        times_transposed(mixed, e1, spread.at[1], tl_own)
        arrived(row_te)

    @pl.when(takes_two)
    def _():
        times(te.at[own, :], fl, mixed)
        times_transposed(mixed, te, tl_own, out_spread.at[1])

    @pl.when(position == count - 2)
    def _():
        out_trans[1] = te[own, :]
        out_spread[1] = tl_own[...]
        out_goff[1] = tg[...]

    @pl.when(position == count - 1)
    def _():
        out_trans[0] = pe[own, :]
        out_spread[0] = pl_own[...]
        out_goff[0] = pg[...]
        out_trans[1] = trans[1]
        out_spread[1] = spread[1]
        out_goff[1] = goff[1]

    left(row_e1 + row_l1 + row_g1 + row_e0 + row_pe)

    @pl.when(gives_two)
    def _():
        left(far_e + far_g + far_l)

    @pl.when(gives_one)
    def _():
        left(next_e + next_g + next_l)

    @pl.when(takes_two)
    def _():
        left(row_fe + row_fg + row_fl)

    @pl.when(takes_one)
    def _():
        left(row_ne + row_ng + row_nl + row_te)


def on_device(count, cores, trans, offset, spread):
    _, rows, width = trans.shape
    kind = trans.dtype
    goff = jnp.broadcast_to(offset[:, None, :], (2, LINES, rows))
    full = pltpu.VMEM((width, width), kind)
    part = pltpu.VMEM((rows, width), kind)
    lines = pltpu.VMEM((cores, LINES, rows), kind)
    line = pltpu.VMEM((LINES, rows), kind)
    n_copies = 10 + 20 * (cores - 1)
    vmem = pl.BlockSpec(memory_space=pltpu.VMEM)
    flops = 12 * 2 * rows * width * width
    a, b, c = pl.pallas_call(
        functools.partial(kernel, count, cores),
        out_shape=(
            jax.ShapeDtypeStruct(trans.shape, kind),
            jax.ShapeDtypeStruct(goff.shape, kind),
            jax.ShapeDtypeStruct(spread.shape, kind),
        ),
        in_specs=[vmem] * 3,
        out_specs=(vmem,) * 3,
        scratch_shapes=[full] * 9 + [part] * 3 + [lines] * 3 + [line] * 2
        + [pltpu.SemaphoreType.DMA((n_copies,)), pltpu.SemaphoreType.DMA((n_copies,))],
        compiler_params=pltpu.CompilerParams(
            collective_id=0, has_side_effects=True, vmem_limit_bytes=56 * 1024 * 1024
        ),
        cost_estimate=pl.CostEstimate(flops=flops, bytes_accessed=4 * trans.size * 2, transcendentals=0),
    )(trans, goff, spread)
    return a, b[:, 0, :], c


def solution(mesh):
    placed = (P("tm", "row", None), P("tm", "row"), P("tm", "row", None))
    body = functools.partial(on_device, mesh.shape["tm"], mesh.shape["row"])
    return jax.shard_map(body, mesh=mesh, in_specs=placed, out_specs=placed, check_vma=False)
```

time: 199 us -> 106 us (0.53)
  waiting for transfers between devices: 113 us -> 0 us
  Pallas kernels: 0 us -> 96.4 us
  matrix products: 37.2 us -> 0 us
  between operations: 14.1 us -> 0.64 us
  starting transfers between devices: 12.3 us -> 0 us
  blocking collectives: 10.1 us -> 0 us
  other arithmetic: 3.62 us -> 0 us
    ppermute x6 -> x0, waiting for transfers between devices: 103 us -> none  [from_later(): return lax.ppermute(block, 'tm', route)]
    pallas_call x0 -> x1, Pallas kernels: none -> 96.4 us  [on_device(): pl.pallas_call(functools.partial(kernel, count, cores), out_shape=(jax.Sh...]
    dot_general x12 -> x0, matrix products: 37.2 us -> none  [the longest x4 22.7 us: compose(): jnp.einsum('ik,jk->ij', partial_value, own_trans_full, preferred_element_...]
    ppermute x6 -> x0, starting transfers between devices: 11.9 us -> none  [from_later(): return lax.ppermute(block, 'tm', route)]
    all_gather x3 -> x0, blocking collectives: 10.1 us -> none  [rows_of_all(): return lax.all_gather(block, 'row', axis=0, tiled=True)]
    all_gather x9 -> x0, waiting for transfers between devices: 8.65 us -> none  [rows_of_all(): return lax.all_gather(block, 'row', axis=0, tiled=True)]
    unnamed x16 -> x5, local copies, waits for them, and re-layouts: 1 us -> 5.13 us
    another operation x3 -> x0, other arithmetic: 3.59 us -> none  [on_device(): return tuple((jnp.stack([a, b]) for a, b in zip(first, second)))]
  transfers between devices with their start and end apart: 15 -> 0, of which waited for: 6 -> 0; matrix products, arithmetic and copies ran while one was open for 19% -> 0% of each run, Pallas kernels for 0% -> 0%
where the time goes in v1:
time: 106 us; the launch traced here: 104 us
  Pallas kernels  96.4 us (91%)
  local copies, waits for them, and re-layouts  7.16 us (7%)
    pallas_call x1, Pallas kernels, on_device(): pl.pallas_call(functools.partial(kernel, count, cores), out_shape=(jax.Sh...  96.4 us
    unnamed x5, local copies, waits for them, and re-layouts  5.13 us

profile of v1, /device:TPU:7, one launch (start us, length us, event | category | flops | bytes accessed | tf_op | source)
XLA Modules:
  0.0 104.2 jit_solution(4704844419495269282)
XLA Ops:
  0.6 1.3 %broadcast_in_dim.2.goff = bf16[2,16,512]{2,1,0:T(8,128)(2,1)} broadcast(bf16[2,512]{1,0:T(2,128)(2,1)} %param.4), dimensions={0,2} | broadcast | bytes 34816 | tf_op jit(solution)/shard_map/broadcast_in_dim | solution.py:278
  1.9 96.4 %shard_map.58 = (bf16[2,512,1024]{2,1,0:T(8,128)(2,1)}, bf16[2,16,512]{2,1,0:T(8,128)(2,1)}, bf16[2,512,1024]{2,1,0:T(8,128)(2,1)}) custom-call(bf16[2,512,1024]{2,1,0:T(8,128)(2,1)} %trans.1, bf16[2,16,512]{2,1,0:T(8,128)(2,1)} %broadcast_in_dim.2.goff, bf16[2,512,1024]{2,1,0:T(8,128)(2,1)} %spread.1), custom_call_target="tpu_custom_call" | custom-call | flops 12884901888 | bytes 8388608 | tf_op jit(solution)/shard_map/pallas_call | solution.py:286
  98.3 0.7 slice.3
  99.1 0.6 copy.8
  99.6 0.0 copy-start
  99.6 3.2 %copy.11 = bf16[2,512,1024]{2,1,0:T(8,128)(2,1)} copy(bf16[2,512,1024]{2,1,0:T(8,128)(2,1)} %get-tuple-element.12) | data formatting | bytes 4194304
  102.9 0.0 copy-done
  102.9 1.3 %copy.12 = bf16[2,512,1024]{2,1,0:T(8,128)(2,1)} copy(bf16[2,512,1024]{2,1,0:T(8,128)(2,1)S(1)} %copy-done) | data formatting | bytes 4194304
Async XLA Ops:
  99.6 3.2 %copy-start = (bf16[2,512,1024]{2,1,0:T(8,128)(2,1)S(1)}, bf16[2,512,1024]{2,1,0:T(8,128)(2,1)}, u32[]{:S(2)}) copy-start(bf16[2,512,1024]{2,1,0:T(8,128)(2,1)} %get-tuple-element.14) | copy-start | bytes 6291460

commit v2 on v1

--- a/solution.py
+++ b/solution.py
@@ -33,7 +33,7 @@
 
 def kernel(
     count, cores, trans, goff, spread, out_trans, out_goff, out_spread,
-    e0, e1, l1, pe, ne, nl, fe, fl, te, mixed, pl_own, tl_own, g1, ng, fg, pg, tg,
+    e0, e1, l1, pe, ne, nl, fe, fl, te, mixed, mixed_far, relay, pl_own, tl_own, g1, ng, fg, pg, tg,
     send_sem, recv_sem,
 ):
     rows, width = trans.shape[1:]
@@ -141,6 +141,10 @@
     far_g = to_device([(goff.at[0], fg.at[core])], two)
     next_e = to_device(spread_rows(ne, whole, pe.at[own, :]), one)
     next_l = to_device(spread_rows(nl, half, pl_own), one)
+    relay_l = to_device(
+        [(pl_own.at[place(a, n), place(b, m)], relay.at[place(a, n), place(b, m)]) for a, n, b, m in half], two
+    )
+    forward_l = to_device(spread_rows(nl, half, relay), {"tm": position + 1})
     next_g = to_device([(pg, ng.at[core])], one)
     row_pe = to_peers(spread_rows(pe, whole))
     row_fe = to_peers(spread_rows(fe, whole))
@@ -155,6 +159,12 @@
     gives_one = position >= 1
     takes_two = position + 2 < count
     takes_one = position + 1 < count
+    even = lax.rem(position, 2) == 0
+    gives_direct = jnp.logical_and(gives_one, jnp.logical_not(even))
+    gives_relay = jnp.logical_and(gives_one, even)
+    forwards = jnp.logical_and(takes_two, even)
+    takes_direct = jnp.logical_and(takes_one, even)
+    takes_forward = jnp.logical_and(takes_one, jnp.logical_not(even))
 
     start(row_e1)
 
@@ -185,7 +195,15 @@
 
     @pl.when(gives_one)
     def _():
-        start(next_g + next_l)
+        start(next_g)
+
+    @pl.when(gives_direct)
+    def _():
+        start(next_l)
+
+    @pl.when(gives_relay)
+    def _():
+        start(relay_l)
 
     arrived(row_pe)
 
@@ -214,17 +232,38 @@
     def _():
         arrived(far_l)
         start(row_fl)
+
+    @pl.when(forwards)
+    def _():
+        for copy, onward in zip(relay_l, forward_l):
+            copy.wait_recv()
+            onward.start()
+
+    @pl.when(takes_two)
+    def _():
         arrived(row_fe)
         times(te.at[own, :], fe, out_trans.at[1])
         arrived(row_fg)
         shift(te.at[own, :], fg, tg, out_goff.at[1])
         arrived(row_fl)
         mirror(fl, cores, rows, width)
+        times(te.at[own, :], fl, mixed_far)
+
+    @pl.when(takes_direct)
+    def _():
+        for copy, onward in zip(next_l, row_nl):
+            copy.wait_recv()
+            onward.start()
+
+    @pl.when(takes_forward)
+    def _():
+        for copy, onward in zip(forward_l, row_nl):
+            copy.wait_recv()
+            onward.start()
 
     @pl.when(takes_one)
     def _():
-        arrived(next_l)
-        start(row_nl)
+        start(row_nl[len(half):])
         arrived(row_nl)
         mirror(nl, cores, rows, width)
         times(pe.at[own, :], nl, mixed)
@@ -235,8 +274,7 @@
 
     @pl.when(takes_two)
     def _():
-        times(te.at[own, :], fl, mixed)
-        times_transposed(mixed, te, tl_own, out_spread.at[1])
+        times_transposed(mixed_far, te, tl_own, out_spread.at[1])
 
     @pl.when(position == count - 2)
     def _():
@@ -261,7 +299,19 @@
 
     @pl.when(gives_one)
     def _():
-        left(next_e + next_g + next_l)
+        left(next_e + next_g)
+
+    @pl.when(gives_direct)
+    def _():
+        left(next_l)
+
+    @pl.when(gives_relay)
+    def _():
+        left(relay_l)
+
+    @pl.when(forwards)
+    def _():
+        left(forward_l)
 
     @pl.when(takes_two)
     def _():
@@ -280,7 +330,7 @@
     part = pltpu.VMEM((rows, width), kind)
     lines = pltpu.VMEM((cores, LINES, rows), kind)
     line = pltpu.VMEM((LINES, rows), kind)
-    n_copies = 10 + 20 * (cores - 1)
+    n_copies = 20 + 20 * (cores - 1)
     vmem = pl.BlockSpec(memory_space=pltpu.VMEM)
     flops = 12 * 2 * rows * width * width
     a, b, c = pl.pallas_call(
@@ -292,7 +342,7 @@
         ),
         in_specs=[vmem] * 3,
         out_specs=(vmem,) * 3,
-        scratch_shapes=[full] * 9 + [part] * 3 + [lines] * 3 + [line] * 2
+        scratch_shapes=[full] * 9 + [part] * 5 + [lines] * 3 + [line] * 2
         + [pltpu.SemaphoreType.DMA((n_copies,)), pltpu.SemaphoreType.DMA((n_copies,))],
         compiler_params=pltpu.CompilerParams(
             collective_id=0, has_side_effects=True, vmem_limit_bytes=56 * 1024 * 1024

time: 106 us -> 108 us (1.019); the launches traced: 104 us -> 108 us
  Pallas kernels: 96.4 us -> 100 us
    pallas_call x1, Pallas kernels: 96.4 us -> 100 us  [on_device(): pl.pallas_call(functools.partial(kernel, count, cores), out_shape=(jax.Sh...]
where the time goes in v2:
time: 108 us
  Pallas kernels  100 us (93%)
  local copies, waits for them, and re-layouts  7.16 us (7%)
    pallas_call x1, Pallas kernels, on_device(): pl.pallas_call(functools.partial(kernel, count, cores), out_shape=(jax.Sh...  100 us
    unnamed x5, local copies, waits for them, and re-layouts  5.13 us

profile of v2, /device:TPU:7, one launch (start us, length us, event | category | flops | bytes accessed | tf_op | source)
XLA Modules:
  0.0 108.0 jit_solution(1466703291492313954)
XLA Ops:
  0.6 1.3 %broadcast_in_dim.2.goff = bf16[2,16,512]{2,1,0:T(8,128)(2,1)} broadcast(bf16[2,512]{1,0:T(2,128)(2,1)} %param.4), dimensions={0,2} | broadcast | bytes 34816 | tf_op jit(solution)/shard_map/broadcast_in_dim | solution.py:328
  1.9 100.2 %shard_map.58 = (bf16[2,512,1024]{2,1,0:T(8,128)(2,1)}, bf16[2,16,512]{2,1,0:T(8,128)(2,1)}, bf16[2,512,1024]{2,1,0:T(8,128)(2,1)}) custom-call(bf16[2,512,1024]{2,1,0:T(8,128)(2,1)} %trans.1, bf16[2,16,512]{2,1,0:T(8,128)(2,1)} %broadcast_in_dim.2.goff, bf16[2,512,1024]{2,1,0:T(8,128)(2,1)} %spread.1), custom_call_target="tpu_custom_call" | custom-call | flops 12884901888 | bytes 8388608 | tf_op jit(solution)/shard_map/pallas_call | solution.py:336
  102.2 0.7 slice.3
  102.9 0.6 copy.8
  103.5 0.0 copy-start
  103.5 3.2 %copy.11 = bf16[2,512,1024]{2,1,0:T(8,128)(2,1)} copy(bf16[2,512,1024]{2,1,0:T(8,128)(2,1)} %get-tuple-element.12) | data formatting | bytes 4194304
  106.7 0.0 copy-done
  106.7 1.3 %copy.12 = bf16[2,512,1024]{2,1,0:T(8,128)(2,1)} copy(bf16[2,512,1024]{2,1,0:T(8,128)(2,1)S(1)} %copy-done) | data formatting | bytes 4194304
Async XLA Ops:
  103.5 3.2 %copy-start = (bf16[2,512,1024]{2,1,0:T(8,128)(2,1)S(1)}, bf16[2,512,1024]{2,1,0:T(8,128)(2,1)}, u32[]{:S(2)}) copy-start(bf16[2,512,1024]{2,1,0:T(8,128)(2,1)} %get-tuple-element.14) | copy-start | bytes 6291460

commit v3 on v2

--- a/solution.py
+++ b/solution.py
@@ -47,8 +47,14 @@
     expected = jnp.int32(cores - 1)
     for _, peer in peers:
         pl.semaphore_signal(barrier, inc=1, device_id={"row": peer}, device_id_type=MESH)
-    for step in (-2, -1, 1, 2):
+    quads = count % 4 == 0
+    quarter = lax.rem(position, 4)
+    for step in (-2, -1, 1, 2) + ((-3, 3) if quads else ()):
         there = jnp.logical_and(position + step >= 0, position + step < count)
+        if step == -3:
+            there = jnp.logical_and(there, quarter == 2)
+        if step == 3:
+            there = jnp.logical_and(there, quarter == 3)
         expected = expected + there.astype(jnp.int32)
 
         @pl.when(there)
@@ -131,6 +137,10 @@
         out[...] = total.astype(jnp.bfloat16)
 
     two = {"tm": position - 2}
+    relay_at, forward_to = position - 2, position + 1
+    if quads:
+        relay_at = jnp.where(quarter == 0, position + 2, position - 2)
+        forward_to = jnp.where(quarter == 0, position + 1, position - 3)
     one = {"tm": position - 1}
     row_e1 = to_peers(spread_rows(e1, whole, trans.at[1]))
     row_l1 = to_peers(spread_rows(l1, whole, spread.at[1]))
@@ -142,9 +152,10 @@
     next_e = to_device(spread_rows(ne, whole, pe.at[own, :]), one)
     next_l = to_device(spread_rows(nl, half, pl_own), one)
     relay_l = to_device(
-        [(pl_own.at[place(a, n), place(b, m)], relay.at[place(a, n), place(b, m)]) for a, n, b, m in half], two
+        [(pl_own.at[place(a, n), place(b, m)], relay.at[place(a, n), place(b, m)]) for a, n, b, m in half],
+        {"tm": relay_at},
     )
-    forward_l = to_device(spread_rows(nl, half, relay), {"tm": position + 1})
+    forward_l = to_device(spread_rows(nl, half, relay), {"tm": forward_to})
     next_g = to_device([(pg, ng.at[core])], one)
     row_pe = to_peers(spread_rows(pe, whole))
     row_fe = to_peers(spread_rows(fe, whole))
@@ -163,6 +174,8 @@
     gives_direct = jnp.logical_and(gives_one, jnp.logical_not(even))
     gives_relay = jnp.logical_and(gives_one, even)
     forwards = jnp.logical_and(takes_two, even)
+    if quads:
+        forwards = jnp.logical_or(quarter == 0, jnp.logical_and(quarter == 2, position > 2))
     takes_direct = jnp.logical_and(takes_one, even)
     takes_forward = jnp.logical_and(takes_one, jnp.logical_not(even))
 

time: 108 us -> 102 us (0.944)
  the two profiles are of different devices: /device:TPU:7 before, /device:TPU:11 now
where the time goes in v3:
time: 102 us
  Pallas kernels  94.3 us (92%)
  local copies, waits for them, and re-layouts  7.16 us (7%)
    pallas_call x1, Pallas kernels, on_device(): pl.pallas_call(functools.partial(kernel, count, cores), out_shape=(jax.Sh...  94.3 us
    unnamed x5, local copies, waits for them, and re-layouts  5.13 us

profile of v3, /device:TPU:11, one launch (start us, length us, event | category | flops | bytes accessed | tf_op | source)
XLA Modules:
  0.0 102.1 jit_solution(13955597422131034303)
XLA Ops:
  0.6 1.3 %broadcast_in_dim.2.goff = bf16[2,16,512]{2,1,0:T(8,128)(2,1)} broadcast(bf16[2,512]{1,0:T(2,128)(2,1)} %param.4), dimensions={0,2} | broadcast | bytes 34816 | tf_op jit(solution)/shard_map/broadcast_in_dim | solution.py:341
  1.9 94.3 %shard_map.58 = (bf16[2,512,1024]{2,1,0:T(8,128)(2,1)}, bf16[2,16,512]{2,1,0:T(8,128)(2,1)}, bf16[2,512,1024]{2,1,0:T(8,128)(2,1)}) custom-call(bf16[2,512,1024]{2,1,0:T(8,128)(2,1)} %trans.1, bf16[2,16,512]{2,1,0:T(8,128)(2,1)} %broadcast_in_dim.2.goff, bf16[2,512,1024]{2,1,0:T(8,128)(2,1)} %spread.1), custom_call_target="tpu_custom_call" | custom-call | flops 12884901888 | bytes 8388608 | tf_op jit(solution)/shard_map/pallas_call | solution.py:349
  96.3 0.7 slice.3
  97.0 0.6 copy.8
  97.6 0.0 copy-start
  97.6 3.2 %copy.11 = bf16[2,512,1024]{2,1,0:T(8,128)(2,1)} copy(bf16[2,512,1024]{2,1,0:T(8,128)(2,1)} %get-tuple-element.12) | data formatting | bytes 4194304
  100.8 0.0 copy-done
  100.8 1.3 %copy.12 = bf16[2,512,1024]{2,1,0:T(8,128)(2,1)} copy(bf16[2,512,1024]{2,1,0:T(8,128)(2,1)S(1)} %copy-done) | data formatting | bytes 4194304
Async XLA Ops:
  97.6 3.2 %copy-start = (bf16[2,512,1024]{2,1,0:T(8,128)(2,1)S(1)}, bf16[2,512,1024]{2,1,0:T(8,128)(2,1)}, u32[]{:S(2)}) copy-start(bf16[2,512,1024]{2,1,0:T(8,128)(2,1)} %get-tuple-element.14) | copy-start | bytes 6291460

commit v4 on v3

--- a/solution.py
+++ b/solution.py
@@ -183,7 +183,7 @@
 
     @pl.when(gives_two)
     def _():
-        start(far_e + far_g + far_l)
+        start(far_e + far_g)
 
     start(row_g1 + row_l1 + row_e0)
     e1[own, :] = trans[1]
@@ -217,6 +217,10 @@
     @pl.when(gives_relay)
     def _():
         start(relay_l)
+
+    @pl.when(gives_two)
+    def _():
+        start(far_l)
 
     arrived(row_pe)
 
@@ -241,11 +245,6 @@
         shift(trans.at[1], ng, goff.at[1], tg)
         shift(pe.at[own, :], ng, pg, out_goff.at[0])
 
-    @pl.when(takes_two)
-    def _():
-        arrived(far_l)
-        start(row_fl)
-
     @pl.when(forwards)
     def _():
         for copy, onward in zip(relay_l, forward_l):
@@ -258,9 +257,6 @@
         times(te.at[own, :], fe, out_trans.at[1])
         arrived(row_fg)
         shift(te.at[own, :], fg, tg, out_goff.at[1])
-        arrived(row_fl)
-        mirror(fl, cores, rows, width)
-        times(te.at[own, :], fl, mixed_far)
 
     @pl.when(takes_direct)
     def _():
@@ -287,6 +283,13 @@
 
     @pl.when(takes_two)
     def _():
+        for copy, onward in zip(far_l, row_fl):
+            copy.wait_recv()
+            onward.start()
+        start(row_fl[len(half):])
+        arrived(row_fl)
+        mirror(fl, cores, rows, width)
+        times(te.at[own, :], fl, mixed_far)
         times_transposed(mixed_far, te, tl_own, out_spread.at[1])
 
     @pl.when(position == count - 2)

time: 102 us -> 101 us (level)
  the two profiles are of different devices: /device:TPU:11 before, /device:TPU:7 now
where the time goes in v4:
time: 101 us
  Pallas kernels  93.4 us (92%)
  local copies, waits for them, and re-layouts  7.16 us (7%)
    pallas_call x1, Pallas kernels, on_device(): pl.pallas_call(functools.partial(kernel, count, cores), out_shape=(jax.Sh...  93.4 us
    unnamed x5, local copies, waits for them, and re-layouts  5.13 us

profile of v4, /device:TPU:7, one launch (start us, length us, event | category | flops | bytes accessed | tf_op | source)
XLA Modules:
  0.0 101.2 jit_solution(4237345642977819355)
XLA Ops:
  0.6 1.3 %broadcast_in_dim.2.goff = bf16[2,16,512]{2,1,0:T(8,128)(2,1)} broadcast(bf16[2,512]{1,0:T(2,128)(2,1)} %param.4), dimensions={0,2} | broadcast | bytes 34816 | tf_op jit(solution)/shard_map/broadcast_in_dim | solution.py:344
  1.9 93.4 %shard_map.58 = (bf16[2,512,1024]{2,1,0:T(8,128)(2,1)}, bf16[2,16,512]{2,1,0:T(8,128)(2,1)}, bf16[2,512,1024]{2,1,0:T(8,128)(2,1)}) custom-call(bf16[2,512,1024]{2,1,0:T(8,128)(2,1)} %trans.1, bf16[2,16,512]{2,1,0:T(8,128)(2,1)} %broadcast_in_dim.2.goff, bf16[2,512,1024]{2,1,0:T(8,128)(2,1)} %spread.1), custom_call_target="tpu_custom_call" | custom-call | flops 12884901888 | bytes 8388608 | tf_op jit(solution)/shard_map/pallas_call | solution.py:352
  95.4 0.7 slice.3
  96.1 0.6 copy.8
  96.7 0.0 copy-start
  96.7 3.2 %copy.11 = bf16[2,512,1024]{2,1,0:T(8,128)(2,1)} copy(bf16[2,512,1024]{2,1,0:T(8,128)(2,1)} %get-tuple-element.12) | data formatting | bytes 4194304
  99.9 0.0 copy-done
  99.9 1.3 %copy.12 = bf16[2,512,1024]{2,1,0:T(8,128)(2,1)} copy(bf16[2,512,1024]{2,1,0:T(8,128)(2,1)S(1)} %copy-done) | data formatting | bytes 4194304
Async XLA Ops:
  96.7 3.2 %copy-start = (bf16[2,512,1024]{2,1,0:T(8,128)(2,1)S(1)}, bf16[2,512,1024]{2,1,0:T(8,128)(2,1)}, u32[]{:S(2)}) copy-start(bf16[2,512,1024]{2,1,0:T(8,128)(2,1)} %get-tuple-element.14) | copy-start | bytes 6291460
